TPU v7x, 256 devices: a whole 4x4x8 slice. The times are simulated.
256 devices in a mesh: gx: 8 (over y, core), gy: 4 (over x), gz: 8 (over z).
Axes of the slice: x: 4, y: 4, z: 8, core: 2. Of those that a mesh axis runs over, the one named last changes fastest.
Arguments:
- fine_old: float32 [1536, 5, 4096], P(('gx', 'gy', 'gz'))
- send_left: int32 [512], P(('gx', 'gy', 'gz')), may hold values from 0 to 5, as said below
- send_right: int32 [512], P(('gx', 'gy', 'gz')), may hold values from 0 to 5
- new_source: int32 [1536], P(('gx', 'gy', 'gz')), may hold values from 0 to 11, as said below
- face_source: int32 [1536, 6], P(('gx', 'gy', 'gz')), may hold values from 0 to 113, as said below
- request_slot: int32 [3584], P(('gx', 'gy', 'gz')), may hold values from 0 to 127, as said below
- request_code: int32 [3584], P(('gx', 'gy', 'gz')), may hold values from 0 to 223, as said below
- coarse_old: float32 [1024, 5, 4096], P(('gx', 'gy', 'gz'))
- coarse_new: float32 [1024, 5, 4096], P(('gx', 'gy', 'gz'))
- coarse_flux: float32 [1024, 6, 5, 256], P(('gx', 'gy', 'gz')), may hold values from -8 to 8
Outputs:
- fine_state: float32 [1536, 5, 4096], P(('gx', 'gy', 'gz'))
- coarse_state: float32 [1024, 5, 4096], P(('gx', 'gy', 'gz'))
Inputs may be any that keep to these rules, and one draw needn't show every extreme that they name: Distinct old slots of one device, none listed in both send_left and send_right. `new_source`: indices into the pool: 6 own old blocks, 2 from the device before, 2 from the device after, then 2 created blocks; no index repeats on a device, every created block is used, and none names a device beyond the ends of the curve. `face_source`: an entry e below 108 names face e % 6, the face opposite, of block e // 6 of the devices before, at and after this one, never beyond the curve's ends; at most 3 entries of a device name the device before and at most 3 the device after, and every device away from the curve's ends has exactly 3 of each; 108 + r names request r, each r below 6 exactly once on a device. `request_slot`: distinct on one device, so at most 4 requests of one device reach one peer; in every draw one peer of each gx group receives 4 from every device of the group. `request_code`: the first 6 of a device are below 96; the last 8 are not, the 4 pieces of one created block in order and to one peer.
All inputs are finite; a program needn't handle non-finite values.
Results may differ from a plain program's by a relative error of at most 0.0003.
Values sent between devices are 32-bit elements; how exact they have to be, the bound alone decides.
A program may use at most 128 MiB of HBM per device.

v0:
```python
import functools

import jax
import jax.numpy as jnp
from jax import lax
from jax.experimental import pallas as pl
from jax.experimental.pallas import tpu as pltpu
from jax.sharding import PartitionSpec as P

MESH = pl.DeviceIdType.MESH
SLOTS = 6
CSLOTS = 4
CAP = 4
FACES = 36
FACEREQ = 6
REQ = 14
NEWB = 2
OCTP = 4
f32 = jnp.float32
i32 = jnp.int32


def pick(x, idx):
    return jnp.take_along_axis(x, idx, axis=1, mode="promise_in_bounds")


def loop(count, body):
    def step(i, carry):
        body(i)
        return carry

    lax.fori_loop(0, count, step, 0)


def lane_of(rows):
    return lax.broadcasted_iota(i32, (rows, 128), 1)


def merge_halves(first, second, rows):
    low = (lane_of(rows) & 15) < 8
    return (
        jnp.where(low, first, pltpu.roll(second, 8, 1)),
        jnp.where(low, pltpu.roll(first, 120, 1), second),
    )


def flux_and_speed(state, axis):
    density, energy = state[0], state[4]
    inverse = 1.0 / density
    kinetic = (state[1] * state[1] + state[2] * state[2] + state[3] * state[3]) * inverse
    pressure = 0.4 * energy - 0.2 * kinetic
    velocity = state[1 + axis] * inverse
    flux = [part * velocity for part in state]
    flux[1 + axis] = flux[1 + axis] + pressure
    flux[4] = flux[4] + pressure * velocity
    return flux, jnp.abs(velocity) + jnp.sqrt(1.4 * pressure * inverse)


def shifted_x(own, ghost_low, ghost_high):
    sub = lax.broadcasted_iota(i32, (4, 8, 128), 1)
    down = pltpu.roll(own, 2, 1)
    entering = pltpu.roll(ghost_low[3], 2, 0)
    low = jnp.where(sub < 2, jnp.concatenate([entering[None], down[:3]], axis=0), down)
    up = pltpu.roll(own, 6, 1)
    entering = pltpu.roll(ghost_high[0], 6, 0)
    high = jnp.where(sub >= 6, jnp.concatenate([up[1:], entering[None]], axis=0), up)
    return low, high


def swap_rows(value, odd):
    return jnp.where(odd, pltpu.roll(value, 1, 1), pltpu.roll(value, 7, 1))


def shifted_y(own, ghost_low, ghost_high):
    odd = (lax.broadcasted_iota(i32, (4, 8, 128), 1) & 1) == 1
    lane = lax.broadcasted_iota(i32, (4, 8, 128), 2)
    low = swap_rows(jnp.where(odd, ghost_low, own), odd)
    low = pltpu.roll(jnp.where(lane >= 112, low, own), 16, 2)
    high = swap_rows(jnp.where(odd, own, ghost_high), odd)
    high = pltpu.roll(jnp.where(lane < 16, high, own), 112, 2)
    return low, high


def shifted_z(own, ghost_low, ghost_high):
    z = lax.broadcasted_iota(i32, (4, 8, 128), 2) & 15
    low = jnp.where(z == 0, pltpu.roll(ghost_low, 113, 2), pltpu.roll(own, 1, 2))
    high = jnp.where(z == 15, pltpu.roll(ghost_high, 15, 2), pltpu.roll(own, 127, 2))
    return low, high


def advance_block(source, put, block, ghost_index):
    shape = (4, 8, 128)
    own = [source[block, c].reshape(shape) for c in range(5)]
    inverse = 1.0 / own[0]
    kinetic = (own[1] * own[1] + own[2] * own[2] + own[3] * own[3]) * inverse
    pressure = 0.4 * own[4] - 0.2 * kinetic
    sound = jnp.sqrt(1.4 * pressure * inverse)
    total = [None] * 5
    for axis, shifted in enumerate((shifted_x, shifted_y, shifted_z)):
        low_at = ghost_index[block * 6 + 2 * axis]
        high_at = ghost_index[block * 6 + 2 * axis + 1]
        low, high = [], []
        for c in range(5):
            below, above = shifted(
                own[c], source[low_at, c].reshape(shape), source[high_at, c].reshape(shape)
            )
            low.append(below)
            high.append(above)
        speed = jnp.abs(own[1 + axis] * inverse) + sound
        low_flux, low_speed = flux_and_speed(low, axis)
        high_flux, high_speed = flux_and_speed(high, axis)
        low_speed = jnp.maximum(low_speed, speed)
        high_speed = jnp.maximum(high_speed, speed)
        for c in range(5):
            part = high_flux[c] - low_flux[c]
            part = part + low_speed * (own[c] - low[c]) - high_speed * (high[c] - own[c])
            total[c] = part if axis == 0 else total[c] + part
    for c in range(5):
        put(block, c, (own[c] - 0.04 * total[c]).reshape(32, 128))


def kernel(
    sizes,
    send_left,
    send_right,
    new_source,
    face_source,
    request_slot,
    request_code,
    fine_hbm,
    old_hbm,
    new_hbm,
    flux_hbm,
    fine_out,
    coarse_out,
    fine_in,
    old_in,
    new_in,
    flux_in,
    codes_out,
    codes_in,
    codes_at,
    wants_out,
    wants_in,
    wants_at,
    ghost_index,
    face_at,
    slot_from,
    face_want,
    own_rows,
    made_rows,
    table_rows,
    own_flat,
    pool,
    moved,
    bundle,
    table,
    payload_out,
    payload_in,
    state_a,
    state_b,
    state_c,
    pick_index,
    pick_mask,
    spread_index,
    grow_index,
    faces_out_a,
    faces_out_b,
    faces_in_a,
    faces_in_b,
    edge_own,
    edge_coarse,
    register,
    average,
    parcel_out,
    parcel_in,
    gathered,
    code_rows,
    load_sem,
    local_sem,
    code_send,
    code_recv,
    want_send,
    want_recv,
    block_send,
    block_recv,
    payload_send,
    payload_recv,
    face_send,
    face_recv,
    parcel_send,
    parcel_recv,
):
    n_gx, n_gy, n_gz = sizes
    peers = n_gy * n_gz
    ranks = n_gx * peers
    gx, gy, gz = lax.axis_index("gx"), lax.axis_index("gy"), lax.axis_index("gz")
    me = gy * n_gz + gz
    rank = gx * peers + me

    def peer_at(step):
        index = lax.rem(me + step, peers)
        return index, (gx, index // n_gz, lax.rem(index, n_gz))

    def on_curve(index):
        return (index // peers, lax.rem(index // n_gz, n_gy), lax.rem(index, n_gz))

    beside = (on_curve(lax.rem(rank + ranks - 1, ranks)), on_curve(lax.rem(rank + 1, ranks)))

    loads = [
        pltpu.make_async_copy(fine_hbm, fine_in, load_sem.at[0]),
        pltpu.make_async_copy(old_hbm, old_in, load_sem.at[1]),
        pltpu.make_async_copy(new_hbm, new_in, load_sem.at[2]),
        pltpu.make_async_copy(flux_hbm, flux_in, load_sem.at[3]),
    ]
    for load in loads:
        load.start()

    faces_out, faces_in = (faces_out_a, faces_out_b), (faces_in_a, faces_in_b)
    barrier = pltpu.get_barrier_semaphore()

    def greet(step):
        pl.semaphore_signal(barrier, inc=1, device_id=peer_at(step + 1)[1], device_id_type=MESH)

    loop(peers - 1, greet)
    for device in beside:
        pl.semaphore_signal(barrier, inc=1, device_id=device, device_id_type=MESH)

    lane1 = lane_of(1)

    def build_codes(peer):
        row = jnp.full((1, 128), -1, i32)
        for r in range(REQ):
            row = jnp.where(lane1 + peer * CAP == request_slot[r], request_code[r], row)
        codes_out[peer] = jnp.where(lane1 < CAP, row, -1)

    loop(peers, build_codes)

    def scan(i, carry):
        count, wants, places = carry
        e = face_source[i // 6, lax.rem(i, 6)]
        is_left = e < FACES
        is_right = (e >= 2 * FACES) & (e < 3 * FACES)
        index = jnp.where(
            is_left,
            SLOTS + jnp.minimum(count[0], 2),
            jnp.where(
                is_right,
                SLOTS + 3 + jnp.minimum(count[1], 2),
                jnp.where(e >= 3 * FACES, SLOTS + 6 + e - 3 * FACES, (e - FACES) // 6),
            ),
        )
        ghost_index[i] = index
        new_wants = tuple(
            jnp.where(is_left & (count[0] == j), e, wants[j]) for j in range(3)
        ) + tuple(
            jnp.where(is_right & (count[1] == j), e - 2 * FACES, wants[3 + j]) for j in range(3)
        )
        new_places = tuple(
            jnp.where(e == 3 * FACES + r, i, places[r]) for r in range(FACEREQ)
        )
        new_count = (
            count[0] + jnp.where(is_left, 1, 0),
            count[1] + jnp.where(is_right, 1, 0),
        )
        return new_count, new_wants, new_places

    zero = jnp.int32(0)
    _, wants, places = lax.fori_loop(
        0, FACES, scan, ((zero, zero), (zero,) * 6, (zero,) * FACEREQ)
    )
    for r in range(FACEREQ):
        face_at[r] = places[r]
    for side in range(2):
        row = jnp.zeros((1, 128), i32)
        for j in range(3):
            row = jnp.where(lane1 == j, wants[3 * side + j], row)
        wants_out[side] = row

    def invert(slot):
        found = jnp.int32(0)
        for r in range(FACEREQ):
            found = jnp.where(request_slot[r] == slot, r, found)
        slot_from[slot] = found

    def rows_of(block, c):
        return pl.ds(pl.multiple_of((block * 5 + c) * 32, 32), 32)

    loads[0].wait()

    def unfold(i):
        c, k = i // 32, lax.rem(i, 32)
        value = fine_in[c, :, pl.ds(pl.multiple_of(k * 128, 128), 128)]
        own_rows[pl.ds(i, SLOTS, stride=160), :] = value

    loop(160, unfold)

    def split_own(block):
        for c in range(5):
            value = own_rows[rows_of(block, c), :]
            own_flat[block, c] = value
            pool[block, c] = value

    loop(SLOTS, split_own)
    for side, listed in enumerate((send_left, send_right)):
        for j in range(2):
            bundle[side, j] = own_flat[listed[j]]

    pl.semaphore_wait(barrier, peers + 1)

    def code_copy(step):
        index, device = peer_at(step)
        return pltpu.make_async_remote_copy(
            src_ref=codes_out.at[index],
            dst_ref=codes_in.at[me],
            send_sem=code_send.at[step],
            recv_sem=code_recv.at[step],
            device_id=device,
            device_id_type=MESH,
        )

    def start_codes(step):
        code_copy(step + 1).start()

    loop(peers - 1, start_codes)

    def beside_copy(side, source, target, send, recv):
        return pltpu.make_async_remote_copy(
            src_ref=source,
            dst_ref=target,
            send_sem=send,
            recv_sem=recv,
            device_id=beside[side],
            device_id_type=MESH,
        )

    want_copies = [
        beside_copy(
            side, wants_out.at[side], wants_in.at[1 - side], want_send.at[side], want_recv.at[1 - side]
        )
        for side in range(2)
    ]
    for copy in want_copies:
        copy.start()
    block_copies = [
        beside_copy(
            side,
            bundle.at[side],
            moved.at[1 - side],
            block_send.at[side],
            block_recv.at[1 - side],
        )
        for side in range(2)
    ]
    for copy in block_copies:
        copy.start()

    loads[1].wait()
    loads[2].wait()
    lane8, lane4 = lane_of(8), lane_of(4)

    def both(c, k):
        at = pl.ds(pl.multiple_of(k * 128, 128), 128)
        return old_in[c, :, at], new_in[c, :, at]

    def put_face(c, face, quadrant, value):
        table_rows[pl.ds((face * 4 + quadrant) * 8 + c, CSLOTS, stride=24 * 8), :] = value

    def fill_table(c):
        for side in range(2):
            for half in range(2):
                first, second = both(c, 30 * side + half)
                for low, value in enumerate(merge_halves(first, second, 4)):
                    put_face(c, side, half * 2 + low, value)
        for side in range(2):

            def fill_y(half, side=side):
                rows = jnp.zeros((8, 128), f32)
                for x in range(8):
                    value = jnp.concatenate(both(c, half * 16 + 2 * x + side), axis=0)
                    shift = (16 * x - 112 * side) % 128
                    value = value if shift == 0 else pltpu.roll(value, shift, 1)
                    rows = jnp.where((lane8 >> 4) == x, value, rows)
                for low, value in enumerate(merge_halves(rows[:4], rows[4:], 4)):
                    put_face(c, 2 + side, half * 2 + low, value)

            loop(2, fill_y)

            def fill_z(quadrant, side=side):
                rows = jnp.zeros((8, 128), f32)
                index = (lane8 & 7) * 16 + 15 * side
                for x in range(8):
                    k = (quadrant // 2) * 16 + 2 * x + lax.rem(quadrant, 2)
                    value = pick(jnp.concatenate(both(c, k), axis=0), index)
                    rows = jnp.where((lane8 >> 4) == x, value, rows)
                put_face(c, 4 + side, quadrant, jnp.where((lane4 & 15) < 8, rows[:4], rows[4:]))

            loop(4, fill_z)

        def fill_octant(i):
            half, pair = i // 8, lax.rem(i, 8)
            at = pl.multiple_of((4 * pair + half) * 128, 128)
            first = old_in[c, :, pl.ds(at, 128)]
            second = old_in[c, :, pl.ds(pl.multiple_of(at + 256, 128), 128)]
            for low, value in enumerate(merge_halves(first, second, 4)):
                code = 96 + ((pair // 4) * 4 + half * 2 + low) * 4 + lax.rem(pair, 4)
                table_rows[pl.ds(code * 8 + c, CSLOTS, stride=32 * 8), :] = value

        loop(16, fill_octant)

    loop(5, fill_table)

    def split_table(code):
        table[code] = table_rows[pl.ds(pl.multiple_of(code * 8, 8), 8), :]

    loop(224, split_table)
    loop(peers * CAP, invert)

    sub = lax.broadcasted_iota(i32, (32, 128), 0)
    lane = lax.broadcasted_iota(i32, (32, 128), 1)
    x, yh = sub >> 1, sub & 1
    for face in range(6):
        axis, side = face // 2, face % 2
        if axis == 0:
            pick_index[face] = lane8
        elif axis == 1:
            pick_index[face] = 112 * side + (lane8 & 15)
        else:
            pick_index[face] = (lane8 & 7) * 16 + 15 * side
        for half in range(2):
            if axis == 0:
                mask = sub == 30 * side + half
            else:
                mask = ((x >> 3) == half) & ((lane >> 4) == (x & 7))
                if axis == 1:
                    mask = mask & (yh == side)
                else:
                    mask = mask & (((lane >> 3) & 1) == yh)
            pick_mask[face, half] = jnp.where(mask, 1.0, 0.0)
    spread_index[0] = lane
    spread_index[1] = (x & 7) * 16 + (lane & 15)
    spread_index[2] = (x & 7) * 16 + 8 * yh + (lane >> 4)
    grow_index[0] = (4 * yh + (lane >> 5)) * 16 + ((lane & 15) >> 1)
    grow_index[1] = (x >> 1) * 16 + ((lane & 15) >> 1)
    grow_index[2] = (x >> 1) * 16 + 4 * yh + (lane >> 5)


    def wait_codes(step):
        code_copy(step + 1).wait()

    loop(peers - 1, wait_codes)
    codes_in[me] = codes_out[me]
    to_scalars = pltpu.make_async_copy(codes_in, codes_at, local_sem.at[0])
    to_scalars.start()
    to_scalars.wait()

    def answer(peer, place):
        code = jnp.maximum(codes_at[peer, 0, place], 0)
        return table[code][:5]

    def payload_copy(step):
        index, device = peer_at(step)
        return pltpu.make_async_remote_copy(
            src_ref=payload_out.at[pl.ds(step * CAP, CAP)],
            dst_ref=payload_in.at[pl.ds(me * CAP, CAP)],
            send_sem=payload_send.at[step],
            recv_sem=payload_recv.at[step],
            device_id=device,
            device_id_type=MESH,
        )

    def start_payload(step):
        index, _ = peer_at(step + 1)
        for place in range(CAP):
            payload_out[(step + 1) * CAP + place] = answer(index, place)
        payload_copy(step + 1).start()

    loop(peers - 1, start_payload)

    for copy in want_copies:
        copy.wait()
    to_scalars = pltpu.make_async_copy(wants_in, wants_at, local_sem.at[1])
    to_scalars.start()
    to_scalars.wait()
    for peer in range(peers):
        code_rows[pl.ds(peer, 1), :] = codes_in[peer]
    for copy in block_copies:
        copy.wait()
    for side in range(2):
        for j in range(2):
            pool[SLOTS + 2 * side + j] = moved[side, j]

    def wait_payload(step):
        payload_copy(step + 1).wait()

    loop(peers - 1, wait_payload)
    for place in range(CAP):
        payload_in[me * CAP + place] = answer(me, place)

    lane5 = lane_of(5)
    grow5 = [(4 * half + (lane5 >> 5)) * 16 + ((lane5 & 15) >> 1) for half in range(2)]
    for block in range(NEWB):
        for piece in range(OCTP):
            value = payload_in[request_slot[FACEREQ + block * OCTP + piece]]
            for part in range(2):
                for half in range(2):
                    grown = pick(value, grow5[half] + 8 * part)
                    for twin in range(2):
                        k = 2 * (4 * piece + 2 * part + twin) + half
                        made_rows[pl.ds(block * 160 + k, 5, stride=32), :] = grown

    for block in range(NEWB):
        for c in range(5):
            pool[10 + block, c] = made_rows[rows_of(block, c), :]

    def regrid(block):
        state_a[block] = pool[new_source[block]]

    loop(SLOTS, regrid)

    def take_face(state, face_id, put):
        block, face = face_id // 6, lax.rem(face_id, 6)
        index = pick_index[face]
        masks = [pick_mask[face, half].reshape(4, 8, 128) for half in range(2)]
        for c in range(5):
            value = state[block, c].reshape(4, 8, 128)
            picked = [pick(value[v], index) for v in range(4)]
            for half in range(2):
                rows = picked[0] * masks[half][0]
                for v in range(1, 4):
                    rows = rows + picked[v] * masks[half][v]
                put(c, half, jnp.sum(rows, axis=0, keepdims=True))

    def send_faces(step, state):
        def one(i):
            side, j = i // 3, lax.rem(i, 3)

            def put(c, half, row):
                faces_out[step][side, j, pl.ds(2 * c + half, 1), :] = row

            take_face(state, wants_at[side, 0, j], put)

        loop(6, one)
        copies = [
            beside_copy(
                side,
                faces_out[step].at[side],
                faces_in[step].at[1 - side],
                face_send.at[step, side],
                face_recv.at[step, 1 - side],
            )
            for side in range(2)
        ]
        for copy in copies:
            copy.start()
        return copies

    def take_edges(state):
        def one(r):
            def put(c, half, row):
                edge_own[c, pl.ds(2 * r + half, 1), :] = row

            take_face(state, face_at[r], put)

        loop(FACEREQ, one)

    def place_faces(step, state):
        def one(i):
            side, j = i // 3, lax.rem(i, 3)
            face = lax.rem(wants_out_face(side, j), 6)
            axis = face // 2
            index = spread_index[axis].reshape(4, 8, 128)
            odd = (lax.broadcasted_iota(i32, (8, 128), 0) & 1) == 1
            for c in range(5):
                first = jnp.broadcast_to(faces_in[step][side, j, pl.ds(2 * c, 1), :], (8, 128))
                second = jnp.broadcast_to(faces_in[step][side, j, pl.ds(2 * c + 1, 1), :], (8, 128))
                both_rows = jnp.where(odd, second, first)
                parts = []
                for v in range(4):
                    rows = jnp.where(axis == 0, both_rows, first if v < 2 else second)
                    parts.append(pick(rows, index[v]))
                state[SLOTS + i, c] = jnp.concatenate(parts, axis=0)

        loop(6, one)

    def wants_out_face(side, j):
        return face_want[side * 3 + j]

    for j in range(6):
        face_want[j] = wants[j]

    def register_step(step):
        axis_row = jnp.zeros((16, 128), i32)
        sign_row = jnp.zeros((16, 128), f32)
        row = lax.broadcasted_iota(i32, (16, 128), 0) >> 1
        for r in range(FACEREQ):
            face = lax.rem(face_at[r], 6)
            axis_row = jnp.where(row == r, face // 2, axis_row)
            sign_row = jnp.where(row == r, (2 * lax.rem(face, 2) - 1).astype(f32), sign_row)
        is_axis = [axis_row == axis for axis in range(3)]
        own = [edge_own[c] for c in range(5)]
        old = [edge_coarse[0, c] for c in range(5)]
        ghost = old
        if step == 1:
            ghost = [old[c] + 0.5 * (edge_coarse[1, c] - old[c]) for c in range(5)]

        def parts(state):
            inverse = 1.0 / state[0]
            normal = jnp.where(is_axis[0], state[1], jnp.where(is_axis[1], state[2], state[3]))
            kinetic = (state[1] * state[1] + state[2] * state[2] + state[3] * state[3]) * inverse
            pressure = 0.4 * state[4] - 0.2 * kinetic
            velocity = normal * inverse
            flux = [part * velocity for part in state]
            for axis in range(3):
                flux[1 + axis] = flux[1 + axis] + jnp.where(is_axis[axis], pressure, 0.0)
            flux[4] = flux[4] + pressure * velocity
            return flux, jnp.abs(velocity) + jnp.sqrt(1.4 * pressure * inverse)

        own_flux, own_speed = parts(own)
        ghost_flux, ghost_speed = parts(ghost)
        speed = jnp.maximum(own_speed, ghost_speed) * sign_row
        for c in range(5):
            value = 0.5 * (own_flux[c] + ghost_flux[c]) - 0.5 * speed * (ghost[c] - own[c])
            at = pl.ds(16 * c, 16)
            register[at, :] = value if step == 0 else register[at, :] + value

    copies = send_faces(0, state_a)
    edge_own[...] = jnp.ones((5, 16, 128), f32)
    edge_coarse[...] = jnp.ones((2, 5, 16, 128), f32)
    take_edges(state_a)

    def coarse_ghosts(r):
        slot = request_slot[r]
        axis = lax.rem(face_at[r], 6) // 2
        index = grow_index[axis].reshape(4, 8, 128)
        value = payload_in[slot]
        for when in range(2):
            for half in range(2):
                grown = pick(value, grow5[half] + 8 * when)
                for c in range(5):
                    edge_coarse[when, c, pl.ds(2 * r + half, 1), :] = grown[c : c + 1]
        for c in range(5):
            rows = jnp.broadcast_to(value[c : c + 1], (8, 128))
            old = jnp.concatenate([pick(rows, index[v]) for v in range(4)], axis=0)
            new = jnp.concatenate([pick(rows, index[v] + 8) for v in range(4)], axis=0)
            state_a[SLOTS + 6 + r, c] = old
            state_b[SLOTS + 6 + r, c] = old + 0.5 * (new - old)

    loop(FACEREQ, coarse_ghosts)
    register_step(0)
    for copy in copies:
        copy.wait()
    place_faces(0, state_a)

    def first_step(block):
        def put(block, c, value):
            state_b[block, c] = value

        advance_block(state_a, put, block, ghost_index)

    loop(SLOTS, first_step)

    copies = send_faces(1, state_b)
    take_edges(state_b)
    register_step(1)

    lane16 = lane_of(16)
    shrink = ((lane16 >> 4) & 3) * 32 + 2 * (lane16 & 7)
    for c in range(5):
        value = register[16 * c : 16 * c + 16, :]
        value = value + pltpu.roll(value, 127, 1)
        value = value + pltpu.roll(value, 112, 1)
        value = value * 0.125
        register[16 * c : 16 * c + 16, :] = jnp.concatenate(
            [pick(value[:8], shrink[:8]), pick(value[8:], shrink[8:])], axis=0
        )
    for r in range(FACEREQ):
        first = register[pl.ds(2 * r, 5, stride=16), :]
        second = register[pl.ds(2 * r + 1, 5, stride=16), :]
        average[r] = jnp.where(lane5 < 64, first, second)

    def parcel_copy(step):
        index, device = peer_at(step)
        return pltpu.make_async_remote_copy(
            src_ref=parcel_out.at[pl.ds(step * 2, 2)],
            dst_ref=parcel_in.at[pl.ds(me * 2, 2)],
            send_sem=parcel_send.at[step],
            recv_sem=parcel_recv.at[step],
            device_id=device,
            device_id_type=MESH,
        )

    def parcel(row):
        first = average[slot_from[2 * row]]
        second = average[slot_from[2 * row + 1]]
        return jnp.where((lane5 & 15) < 8, first, second)

    def start_parcel(step):
        index, _ = peer_at(step + 1)
        for pair in range(2):
            parcel_out[(step + 1) * 2 + pair] = parcel(index * 2 + pair)
        parcel_copy(step + 1).start()

    loop(peers - 1, start_parcel)

    for copy in copies:
        copy.wait()
    place_faces(1, state_b)

    def second_step(block):
        def put(block, c, value):
            state_c[rows_of(block, c), :] = value

        advance_block(state_b, put, block, ghost_index)

    loop(SLOTS, second_step)

    def fold(i):
        c, k = i // 32, lax.rem(i, 32)
        value = state_c[pl.ds(i, SLOTS, stride=160), :]
        fine_out[c, :, pl.ds(pl.multiple_of(k * 128, 128), 128)] = value

    loop(160, fold)

    target = lax.broadcasted_iota(i32, (peers, 128), 1)
    wanted = jnp.where(target < 24 * CSLOTS, (target & 3) * 24 + (target >> 2), -7)
    chosen = []
    for half in range(2):
        picks = [
            (jnp.broadcast_to(code_rows[:, 2 * pair + half : 2 * pair + half + 1], (peers, 128)) == wanted)
            for pair in range(2)
        ]
        chosen.append(
            jnp.concatenate([jnp.where(p, 1.0, 0.0) for p in picks], axis=0).astype(jnp.bfloat16)
        )

    def contract(left, right):
        return lax.dot_general(
            left, right, (((0,), (0,)), ((), ())), preferred_element_type=f32
        )

    ones = jnp.ones((2 * peers, 128), jnp.bfloat16)
    counts = contract(chosen[0], ones) + contract(chosen[1], ones)
    loads[3].wait()

    def wait_parcel(step):
        parcel_copy(step + 1).wait()

    loop(peers - 1, wait_parcel)
    for pair in range(2):
        parcel_in[me * 2 + pair] = parcel(me * 2 + pair)

    def line_up(peer):
        for pair in range(2):
            gathered[pl.ds(pair * peers + peer, 5, stride=2 * peers), :] = parcel_in[peer * 2 + pair]

    loop(peers, line_up)
    low8, low4 = (lane8 & 15) < 8, (lane4 & 15) < 8
    for c in range(5):
        value = gathered[pl.ds(c * 2 * peers, 2 * peers), :]
        coarse_part = value.astype(jnp.bfloat16)
        rest = (value - coarse_part.astype(f32)).astype(jnp.bfloat16)
        sums = [contract(chosen[h], coarse_part) + contract(chosen[h], rest) for h in range(2)]
        change = {}
        for face in range(6):
            scale = 0.08 if face % 2 else -0.08
            for half in range(2):
                at = (face * 2 + half) * 8
                first, second = sums[0][at : at + 8], sums[1][at : at + 8]
                count = counts[at : at + 8]
                lows = first + pltpu.roll(second, 120, 1)
                highs = second + pltpu.roll(first, 8, 1)
                total = jnp.where(low4, lows[:4], highs[4:])
                number = jnp.where(low4, count[:4], count[4:])
                flux = flux_in[face, c, :, pl.ds(half * 128, 128)]
                change[face, half] = scale * (number * flux - total)
        stacked = {
            face: jnp.concatenate([change[face, 0], change[face, 1]], axis=0) for face in range(2, 6)
        }
        for x8 in range(8):
            for yh8 in range(2):
                shift = (112 * yh8 - 16 * x8) % 128
                moved = stacked[2 + yh8]
                moved = moved if shift == 0 else pltpu.roll(moved, shift, 1)
                added = jnp.where((lane8 >> 4) == 7 * yh8, moved, 0.0)
                index = x8 * 16 + 8 * yh8 + (lane8 >> 4)
                added = added + jnp.where((lane8 & 15) == 0, pick(stacked[4], index), 0.0)
                added = added + jnp.where((lane8 & 15) == 15, pick(stacked[5], index), 0.0)
                for upper in range(2):
                    x_at = 8 * upper + x8
                    at = pl.ds((2 * x_at + yh8) * 128, 128)
                    value = new_in[c, :, at] + added[4 * upper : 4 * upper + 4]
                    if x_at == 0:
                        value = value + change[0, yh8]
                    if x_at == 15:
                        value = value + change[1, yh8]
                    coarse_out[c, :, at] = value


def on_device(sizes, fine_old, send_left, send_right, new_source, face_source, request_slot, request_code,
              coarse_old, coarse_new, coarse_flux):
    peers = sizes[1] * sizes[2]
    smem = pl.BlockSpec(memory_space=pltpu.SMEM)
    vmem = pl.BlockSpec(memory_space=pltpu.VMEM)
    hbm = pl.BlockSpec(memory_space=pl.ANY)
    dma = pltpu.SemaphoreType.DMA
    V = pltpu.VMEM
    fine, coarse = pl.pallas_call(
        functools.partial(kernel, sizes),
        out_shape=(
            jax.ShapeDtypeStruct((5, SLOTS, 4096), f32),
            jax.ShapeDtypeStruct((5, CSLOTS, 4096), f32),
        ),
        in_specs=[smem] * 6 + [hbm] * 4,
        out_specs=(vmem, vmem),
        scratch_shapes=[
            V((5, SLOTS, 4096), f32),
            V((5, CSLOTS, 4096), f32),
            V((5, CSLOTS, 4096), f32),
            V((6, 5, CSLOTS, 256), f32),
            V((peers, 1, 128), i32),
            V((peers, 1, 128), i32),
            pltpu.SMEM((peers, 1, 128), i32),
            V((2, 1, 128), i32),
            V((2, 1, 128), i32),
            pltpu.SMEM((2, 1, 128), i32),
            pltpu.SMEM((FACES,), i32),
            pltpu.SMEM((8,), i32),
            pltpu.SMEM((peers * CAP,), i32),
            pltpu.SMEM((8,), i32),
            V((8 * 160, 128), f32),
            V((416, 128), f32),
            V((2816, 128), f32),
            V((SLOTS, 5, 32, 128), f32),
            V((12, 5, 32, 128), f32),
            V((2, 2, 5, 32, 128), f32),
            V((2, 2, 5, 32, 128), f32),
            V((224, 8, 128), f32),
            V((peers * CAP, 5, 128), f32),
            V((peers * CAP, 5, 128), f32),
            V((18, 5, 32, 128), f32),
            V((18, 5, 32, 128), f32),
            V((8 * 160, 128), f32),
            V((6, 8, 128), i32),
            V((6, 2, 32, 128), f32),
            V((3, 32, 128), i32),
            V((3, 32, 128), i32),
            V((2, 3, 10, 128), f32),
            V((2, 3, 10, 128), f32),
            V((2, 3, 10, 128), f32),
            V((2, 3, 10, 128), f32),
            V((5, 16, 128), f32),
            V((2, 5, 16, 128), f32),
            V((128, 128), f32),
            V((FACEREQ, 5, 128), f32),
            V((peers * 2, 5, 128), f32),
            V((peers * 2, 5, 128), f32),
            V((8 * 2 * peers, 128), f32),
            V((peers, 128), i32),
            dma((4,)),
            dma((2,)),
            dma((peers,)),
            dma((peers,)),
            dma((2,)),
            dma((2,)),
            dma((2,)),
            dma((2,)),
            dma((peers,)),
            dma((peers,)),
            dma((2, 2)),
            dma((2, 2)),
            dma((peers,)),
            dma((peers,)),
        ],
        compiler_params=pltpu.CompilerParams(
            collective_id=0, has_side_effects=True, vmem_limit_bytes=40 * 1024 * 1024
        ),
    )(
        send_left,
        send_right,
        new_source,
        face_source,
        request_slot,
        request_code,
        jnp.transpose(fine_old, (1, 0, 2)),
        jnp.transpose(coarse_old, (1, 0, 2)),
        jnp.transpose(coarse_new, (1, 0, 2)),
        jnp.transpose(coarse_flux, (1, 2, 0, 3)),
    )
    return jnp.transpose(fine, (1, 0, 2)), jnp.transpose(coarse, (1, 0, 2))


def solution(mesh):
    sizes = (mesh.shape["gx"], mesh.shape["gy"], mesh.shape["gz"])
    every = ("gx", "gy", "gz")
    in_specs = (
        P(every, None, None),
        P(every),
        P(every),
        P(every),
        P(every, None),
        P(every),
        P(every),
        P(every, None, None),
        P(every, None, None),
        P(every, None, None, None),
    )
    out_specs = (P(every, None, None), P(every, None, None))
    return jax.shard_map(
        functools.partial(on_device, sizes), mesh=mesh, in_specs=in_specs, out_specs=out_specs, check_vma=False
    )
```

profile of v0, /device:TPU:1, one launch (start us, length us, event | category | flops | bytes accessed | tf_op | source)
XLA Modules:
  0.0 66.3 jit_solution(13766477551963011661)
XLA Ops:
  0.6 0.0 copy-start.4
  0.6 0.0 copy-start.8
  0.7 0.0 copy-start.9
  0.7 0.0 copy-start.5
  0.7 0.0 copy-start.6
  0.7 0.0 copy-start.7
  0.7 0.6 copy-done.4
  1.3 0.0 copy-done.8
  1.3 0.0 copy-done.9
  1.3 0.0 copy-done.5
  1.3 0.0 copy-done.6
  1.4 0.0 copy-done.7
  1.4 0.0 copy-start
  1.4 1.1 %copy-done = f32[6,5,4096]{2,0,1:T(8,128)S(1)} copy-done((f32[6,5,4096]{2,0,1:T(8,128)S(1)}, f32[6,5,4096]{2,0,1:T(8,128)}, u32[]{:S(2)}) %copy-start) | copy-done | bytes 491544
  2.5 0.0 copy-start.1
  2.5 1.0 %copy-done.1 = f32[4,5,4096]{2,0,1:T(4,128)S(1)} copy-done((f32[4,5,4096]{2,0,1:T(4,128)S(1)}, f32[4,5,4096]{2,0,1:T(4,128)}, u32[]{:S(2)}) %copy-start.1) | copy-done | bytes 327704
  3.4 0.0 copy-start.2
  3.4 1.0 %copy-done.2 = f32[4,5,4096]{2,0,1:T(4,128)S(1)} copy-done((f32[4,5,4096]{2,0,1:T(4,128)S(1)}, f32[4,5,4096]{2,0,1:T(4,128)}, u32[]{:S(2)}) %copy-start.2) | copy-done | bytes 327704
  4.4 0.0 copy-start.3
  4.4 0.9 %copy-done.3 = f32[4,6,5,256]{3,0,2,1:T(4,128)S(1)} copy-done((f32[4,6,5,256]{3,0,2,1:T(4,128)S(1)}, f32[4,6,5,256]{3,0,2,1:T(4,128)}, u32[]{:S(2)}) %copy-start.3) | copy-done | bytes 122904
  5.3 59.4 %shard_map.113 = (f32[5,6,4096]{2,1,0:T(8,128)S(1)}, f32[5,4,4096]{2,1,0:T(4,128)S(1)}) custom-call(s32[2]{0:T(128)S(1)} %copy-done.5, s32[2]{0:T(128)S(1)} %copy-done.6, s32[6]{0:T(128)S(1)} %copy-done.7, s32[6,6]{1,0:T(8,128)S(1)} %copy-done.4, s32[14]{0:T(128)S(1)} %copy-done.8, s32[14]{0:T(128)S(1)} %copy-done.9, f32[5,6,4096]{2,1,0:T(8,128)S(1)} %bitcast.6, ...), custom_call_target="tpu_custom_call" | custom-call | tf_op jit(solution)/shard_map/pallas_call | solution.py:808
  64.7 0.8 %copy.14 = f32[6,5,4096]{2,0,1:T(8,128)} copy(f32[6,5,4096]{2,0,1:T(8,128)S(1)} %bitcast.7) | data formatting | bytes 983040
  65.6 0.7 %copy.15 = f32[4,5,4096]{2,0,1:T(4,128)} copy(f32[4,5,4096]{2,0,1:T(4,128)S(1)} %bitcast.8) | data formatting | bytes 655360
Async XLA Ops:
  0.6 0.7 %copy-start.4 = (s32[6,6]{1,0:T(8,128)S(1)}, s32[6,6]{1,0:T(8,128)}, u32[]{:S(2)}) copy-start(s32[6,6]{1,0:T(8,128)} %face_source.1) | copy-start | bytes 436
  0.6 0.7 %copy-start.8 = (s32[14]{0:T(128)S(1)}, s32[14]{0:T(128)}, u32[]{:S(2)}) copy-start(s32[14]{0:T(128)} %request_slot.1) | copy-start | bytes 172
  0.7 0.7 %copy-start.9 = (s32[14]{0:T(128)S(1)}, s32[14]{0:T(128)}, u32[]{:S(2)}) copy-start(s32[14]{0:T(128)} %request_code.1) | copy-start | bytes 172
  0.7 0.7 %copy-start.5 = (s32[2]{0:T(128)S(1)}, s32[2]{0:T(128)}, u32[]{:S(2)}) copy-start(s32[2]{0:T(128)} %send_left.1) | copy-start | bytes 28
  0.7 0.7 %copy-start.6 = (s32[2]{0:T(128)S(1)}, s32[2]{0:T(128)}, u32[]{:S(2)}) copy-start(s32[2]{0:T(128)} %send_right.1) | copy-start | bytes 28
  0.7 0.7 %copy-start.7 = (s32[6]{0:T(128)S(1)}, s32[6]{0:T(128)}, u32[]{:S(2)}) copy-start(s32[6]{0:T(128)} %new_source.1) | copy-start | bytes 76
  1.4 1.1 %copy-start = (f32[6,5,4096]{2,0,1:T(8,128)S(1)}, f32[6,5,4096]{2,0,1:T(8,128)}, u32[]{:S(2)}) copy-start(f32[6,5,4096]{2,0,1:T(8,128)} %param.10) | copy-start | bytes 1474564
  2.5 1.0 %copy-start.1 = (f32[4,5,4096]{2,0,1:T(4,128)S(1)}, f32[4,5,4096]{2,0,1:T(4,128)}, u32[]{:S(2)}) copy-start(f32[4,5,4096]{2,0,1:T(4,128)} %param.17) | copy-start | bytes 983044
  3.4 1.0 %copy-start.2 = (f32[4,5,4096]{2,0,1:T(4,128)S(1)}, f32[4,5,4096]{2,0,1:T(4,128)}, u32[]{:S(2)}) copy-start(f32[4,5,4096]{2,0,1:T(4,128)} %param.18) | copy-start | bytes 983044
  4.4 0.9 %copy-start.3 = (f32[4,6,5,256]{3,0,2,1:T(4,128)S(1)}, f32[4,6,5,256]{3,0,2,1:T(4,128)}, u32[]{:S(2)}) copy-start(f32[4,6,5,256]{3,0,2,1:T(4,128)} %param.19) | copy-start | bytes 368644
where the time goes:
time: 66.5 us; the launch traced here: 66.3 us
  Pallas kernels  59.4 us (89%)
  local copies, waits for them, and re-layouts  6.18 us (9%)
  between operations  0.7 us (1%)
    pallas_call x1, Pallas kernels, on_device(): pl.pallas_call(functools.partial(kernel, sizes), out_shape=(jax.ShapeDtyp...  59.4 us
    unnamed x22, local copies, waits for them, and re-layouts  6.18 us

commit v1 on v0

--- a/solution.py
+++ b/solution.py
@@ -24,12 +24,15 @@
     return jnp.take_along_axis(x, idx, axis=1, mode="promise_in_bounds")
 
 
-def loop(count, body):
+def loop(count, body, unroll=1):
     def step(i, carry):
+        for part in range(unroll):
+            body(i * unroll + part)
+        return carry
+
+    lax.fori_loop(0, count // unroll, step, 0)
+    for i in range(count - count % unroll, count):
         body(i)
-        return carry
-
-    lax.fori_loop(0, count, step, 0)
 
 
 def lane_of(rows):
@@ -200,12 +203,23 @@
 
     def peer_at(step):
         index = lax.rem(me + step, peers)
-        return index, (gx, index // n_gz, lax.rem(index, n_gz))
+        return index, (gx, lax.div(index, n_gz), lax.rem(index, n_gz))
 
     def on_curve(index):
-        return (index // peers, lax.rem(index // n_gz, n_gy), lax.rem(index, n_gz))
+        return (lax.div(index, peers), lax.rem(lax.div(index, n_gz), n_gy), lax.rem(index, n_gz))
 
     beside = (on_curve(lax.rem(rank + ranks - 1, ranks)), on_curve(lax.rem(rank + 1, ranks)))
+
+    faces_out, faces_in = (faces_out_a, faces_out_b), (faces_in_a, faces_in_b)
+    barrier = pltpu.get_barrier_semaphore()
+
+    def greet(step):
+        pl.semaphore_signal(barrier, inc=1, device_id=peer_at(step + 1)[1], device_id_type=MESH)
+
+    for step in range(peers - 1):
+        greet(step)
+    for device in beside:
+        pl.semaphore_signal(barrier, inc=1, device_id=device, device_id_type=MESH)
 
     loads = [
         pltpu.make_async_copy(fine_hbm, fine_in, load_sem.at[0]),
@@ -216,29 +230,178 @@
     for load in loads:
         load.start()
 
-    faces_out, faces_in = (faces_out_a, faces_out_b), (faces_in_a, faces_in_b)
-    barrier = pltpu.get_barrier_semaphore()
-
-    def greet(step):
-        pl.semaphore_signal(barrier, inc=1, device_id=peer_at(step + 1)[1], device_id_type=MESH)
-
-    loop(peers - 1, greet)
-    for device in beside:
-        pl.semaphore_signal(barrier, inc=1, device_id=device, device_id_type=MESH)
-
     lane1 = lane_of(1)
-
-    def build_codes(peer):
-        row = jnp.full((1, 128), -1, i32)
-        for r in range(REQ):
-            row = jnp.where(lane1 + peer * CAP == request_slot[r], request_code[r], row)
-        codes_out[peer] = jnp.where(lane1 < CAP, row, -1)
-
-    loop(peers, build_codes)
+    place_of = lax.broadcasted_iota(i32, (peers, 128), 0) * CAP + lane_of(peers)
+    rows = jnp.full((peers, 128), -1, i32)
+    for r in range(REQ):
+        rows = jnp.where(place_of == request_slot[r], request_code[r], rows)
+    code_rows[...] = jnp.where(lane_of(peers) < CAP, rows, -1)
+    for peer in range(peers):
+        codes_out[peer] = code_rows[pl.ds(peer, 1), :]
+
+    pl.semaphore_wait(barrier, peers + 1)
+
+    def code_copy(step):
+        index, device = peer_at(step)
+        return pltpu.make_async_remote_copy(
+            src_ref=codes_out.at[index],
+            dst_ref=codes_in.at[me],
+            send_sem=code_send.at[step],
+            recv_sem=code_recv.at[step],
+            device_id=device,
+            device_id_type=MESH,
+        )
+
+    def start_codes(step):
+        code_copy(step + 1).start()
+
+    for step in range(peers - 1):
+        start_codes(step)
+
+    def rows_of(block, c):
+        return pl.ds(pl.multiple_of((block * 5 + c) * 32, 32), 32)
+
+    loads[0].wait()
+
+    def unfold(i):
+        c, k = lax.div(i, 32), lax.rem(i, 32)
+        value = fine_in[c, :, pl.ds(pl.multiple_of(k * 128, 128), 128)]
+        own_rows[pl.ds(i, SLOTS, stride=160), :] = value
+
+    loop(160, unfold, 16)
+
+    def split_own(block):
+        for c in range(5):
+            value = own_rows[rows_of(block, c), :]
+            own_flat[block, c] = value
+            pool[block, c] = value
+
+    loop(SLOTS, split_own, 2)
+    for side, listed in enumerate((send_left, send_right)):
+        for j in range(2):
+            bundle[side, j] = own_flat[listed[j]]
+
+    def beside_copy(side, source, target, send, recv):
+        return pltpu.make_async_remote_copy(
+            src_ref=source,
+            dst_ref=target,
+            send_sem=send,
+            recv_sem=recv,
+            device_id=beside[side],
+            device_id_type=MESH,
+        )
+
+    block_copies = [
+        beside_copy(
+            side,
+            bundle.at[side],
+            moved.at[1 - side],
+            block_send.at[side],
+            block_recv.at[1 - side],
+        )
+        for side in range(2)
+    ]
+    for copy in block_copies:
+        copy.start()
+
+    loads[1].wait()
+    loads[2].wait()
+    lane8, lane4 = lane_of(8), lane_of(4)
+
+    def both(c, k):
+        at = pl.ds(k * 128, 128)
+        return old_in[c, :, at], new_in[c, :, at]
+
+    def put_face(c, face, quadrant, value):
+        table_rows[pl.ds((face * 4 + quadrant) * 8 + c, CSLOTS, stride=24 * 8), :] = value
+
+    def fill_table(c):
+        for side in range(2):
+            for half in range(2):
+                first, second = both(c, 30 * side + half)
+                for low, value in enumerate(merge_halves(first, second, 4)):
+                    put_face(c, side, half * 2 + low, value)
+        for side in range(2):
+
+            def fill_y(half, side=side):
+                rows = jnp.zeros((8, 128), f32)
+                for x in range(8):
+                    value = jnp.concatenate(both(c, half * 16 + 2 * x + side), axis=0)
+                    shift = (16 * x - 112 * side) % 128
+                    value = value if shift == 0 else pltpu.roll(value, shift, 1)
+                    rows = jnp.where((lane8 >> 4) == x, value, rows)
+                for low, value in enumerate(merge_halves(rows[:4], rows[4:], 4)):
+                    put_face(c, 2 + side, half * 2 + low, value)
+
+            for half in range(2):
+                fill_y(half)
+
+            def fill_z(quadrant, side=side):
+                rows = jnp.zeros((8, 128), f32)
+                index = (lane8 & 7) * 16 + 15 * side
+                for x in range(8):
+                    k = (quadrant // 2) * 16 + 2 * x + quadrant % 2
+                    value = pick(jnp.concatenate(both(c, k), axis=0), index)
+                    rows = jnp.where((lane8 >> 4) == x, value, rows)
+                put_face(c, 4 + side, quadrant, jnp.where((lane4 & 15) < 8, rows[:4], rows[4:]))
+
+            for quadrant in range(4):
+                fill_z(quadrant)
+
+        def fill_octant(i):
+            half, pair = i // 8, i % 8
+            at = (4 * pair + half) * 128
+            first = old_in[c, :, pl.ds(at, 128)]
+            second = old_in[c, :, pl.ds(at + 256, 128)]
+            for low, value in enumerate(merge_halves(first, second, 4)):
+                code = 96 + ((pair // 4) * 4 + half * 2 + low) * 4 + pair % 4
+                table_rows[pl.ds(code * 8 + c, CSLOTS, stride=32 * 8), :] = value
+
+        for i in range(16):
+            fill_octant(i)
+
+    loop(5, fill_table)
+
+    def split_table(code):
+        table[code] = table_rows[pl.ds(pl.multiple_of(code * 8, 8), 8), :]
+
+    loop(224, split_table, 16)
+
+    def wait_codes(step):
+        code_copy(step + 1).wait()
+
+    loop(peers - 1, wait_codes)
+    codes_in[me] = codes_out[me]
+    to_scalars = pltpu.make_async_copy(codes_in, codes_at, local_sem.at[0])
+    to_scalars.start()
+    to_scalars.wait()
+
+    def answer(peer, place):
+        code = jnp.maximum(codes_at[peer, 0, place], 0)
+        return table[code][:5]
+
+    def payload_copy(step):
+        index, device = peer_at(step)
+        return pltpu.make_async_remote_copy(
+            src_ref=payload_out.at[pl.ds(step * CAP, CAP)],
+            dst_ref=payload_in.at[pl.ds(me * CAP, CAP)],
+            send_sem=payload_send.at[step],
+            recv_sem=payload_recv.at[step],
+            device_id=device,
+            device_id_type=MESH,
+        )
+
+    def start_payload(step):
+        index, _ = peer_at(step + 1)
+        for place in range(CAP):
+            payload_out[(step + 1) * CAP + place] = answer(index, place)
+        payload_copy(step + 1).start()
+
+    loop(peers - 1, start_payload, 4)
 
     def scan(i, carry):
         count, wants, places = carry
-        e = face_source[i // 6, lax.rem(i, 6)]
+        e = face_source[lax.div(i, 6), lax.rem(i, 6)]
         is_left = e < FACES
         is_right = (e >= 2 * FACES) & (e < 3 * FACES)
         index = jnp.where(
@@ -247,7 +410,7 @@
             jnp.where(
                 is_right,
                 SLOTS + 3 + jnp.minimum(count[1], 2),
-                jnp.where(e >= 3 * FACES, SLOTS + 6 + e - 3 * FACES, (e - FACES) // 6),
+                jnp.where(e >= 3 * FACES, SLOTS + 6 + e - 3 * FACES, lax.div(jnp.maximum(e - FACES, 0), 6)),
             ),
         )
         ghost_index[i] = index
@@ -283,57 +446,6 @@
             found = jnp.where(request_slot[r] == slot, r, found)
         slot_from[slot] = found
 
-    def rows_of(block, c):
-        return pl.ds(pl.multiple_of((block * 5 + c) * 32, 32), 32)
-
-    loads[0].wait()
-
-    def unfold(i):
-        c, k = i // 32, lax.rem(i, 32)
-        value = fine_in[c, :, pl.ds(pl.multiple_of(k * 128, 128), 128)]
-        own_rows[pl.ds(i, SLOTS, stride=160), :] = value
-
-    loop(160, unfold)
-
-    def split_own(block):
-        for c in range(5):
-            value = own_rows[rows_of(block, c), :]
-            own_flat[block, c] = value
-            pool[block, c] = value
-
-    loop(SLOTS, split_own)
-    for side, listed in enumerate((send_left, send_right)):
-        for j in range(2):
-            bundle[side, j] = own_flat[listed[j]]
-
-    pl.semaphore_wait(barrier, peers + 1)
-
-    def code_copy(step):
-        index, device = peer_at(step)
-        return pltpu.make_async_remote_copy(
-            src_ref=codes_out.at[index],
-            dst_ref=codes_in.at[me],
-            send_sem=code_send.at[step],
-            recv_sem=code_recv.at[step],
-            device_id=device,
-            device_id_type=MESH,
-        )
-
-    def start_codes(step):
-        code_copy(step + 1).start()
-
-    loop(peers - 1, start_codes)
-
-    def beside_copy(side, source, target, send, recv):
-        return pltpu.make_async_remote_copy(
-            src_ref=source,
-            dst_ref=target,
-            send_sem=send,
-            recv_sem=recv,
-            device_id=beside[side],
-            device_id_type=MESH,
-        )
-
     want_copies = [
         beside_copy(
             side, wants_out.at[side], wants_in.at[1 - side], want_send.at[side], want_recv.at[1 - side]
@@ -342,80 +454,6 @@
     ]
     for copy in want_copies:
         copy.start()
-    block_copies = [
-        beside_copy(
-            side,
-            bundle.at[side],
-            moved.at[1 - side],
-            block_send.at[side],
-            block_recv.at[1 - side],
-        )
-        for side in range(2)
-    ]
-    for copy in block_copies:
-        copy.start()
-
-    loads[1].wait()
-    loads[2].wait()
-    lane8, lane4 = lane_of(8), lane_of(4)
-
-    def both(c, k):
-        at = pl.ds(pl.multiple_of(k * 128, 128), 128)
-        return old_in[c, :, at], new_in[c, :, at]
-
-    def put_face(c, face, quadrant, value):
-        table_rows[pl.ds((face * 4 + quadrant) * 8 + c, CSLOTS, stride=24 * 8), :] = value
-
-    def fill_table(c):
-        for side in range(2):
-            for half in range(2):
-                first, second = both(c, 30 * side + half)
-                for low, value in enumerate(merge_halves(first, second, 4)):
-                    put_face(c, side, half * 2 + low, value)
-        for side in range(2):
-
-            def fill_y(half, side=side):
-                rows = jnp.zeros((8, 128), f32)
-                for x in range(8):
-                    value = jnp.concatenate(both(c, half * 16 + 2 * x + side), axis=0)
-                    shift = (16 * x - 112 * side) % 128
-                    value = value if shift == 0 else pltpu.roll(value, shift, 1)
-                    rows = jnp.where((lane8 >> 4) == x, value, rows)
-                for low, value in enumerate(merge_halves(rows[:4], rows[4:], 4)):
-                    put_face(c, 2 + side, half * 2 + low, value)
-
-            loop(2, fill_y)
-
-            def fill_z(quadrant, side=side):
-                rows = jnp.zeros((8, 128), f32)
-                index = (lane8 & 7) * 16 + 15 * side
-                for x in range(8):
-                    k = (quadrant // 2) * 16 + 2 * x + lax.rem(quadrant, 2)
-                    value = pick(jnp.concatenate(both(c, k), axis=0), index)
-                    rows = jnp.where((lane8 >> 4) == x, value, rows)
-                put_face(c, 4 + side, quadrant, jnp.where((lane4 & 15) < 8, rows[:4], rows[4:]))
-
-            loop(4, fill_z)
-
-        def fill_octant(i):
-            half, pair = i // 8, lax.rem(i, 8)
-            at = pl.multiple_of((4 * pair + half) * 128, 128)
-            first = old_in[c, :, pl.ds(at, 128)]
-            second = old_in[c, :, pl.ds(pl.multiple_of(at + 256, 128), 128)]
-            for low, value in enumerate(merge_halves(first, second, 4)):
-                code = 96 + ((pair // 4) * 4 + half * 2 + low) * 4 + lax.rem(pair, 4)
-                table_rows[pl.ds(code * 8 + c, CSLOTS, stride=32 * 8), :] = value
-
-        loop(16, fill_octant)
-
-    loop(5, fill_table)
-
-    def split_table(code):
-        table[code] = table_rows[pl.ds(pl.multiple_of(code * 8, 8), 8), :]
-
-    loop(224, split_table)
-    loop(peers * CAP, invert)
-
     sub = lax.broadcasted_iota(i32, (32, 128), 0)
     lane = lax.broadcasted_iota(i32, (32, 128), 1)
     x, yh = sub >> 1, sub & 1
@@ -444,38 +482,7 @@
     grow_index[1] = (x >> 1) * 16 + ((lane & 15) >> 1)
     grow_index[2] = (x >> 1) * 16 + 4 * yh + (lane >> 5)
 
-
-    def wait_codes(step):
-        code_copy(step + 1).wait()
-
-    loop(peers - 1, wait_codes)
-    codes_in[me] = codes_out[me]
-    to_scalars = pltpu.make_async_copy(codes_in, codes_at, local_sem.at[0])
-    to_scalars.start()
-    to_scalars.wait()
-
-    def answer(peer, place):
-        code = jnp.maximum(codes_at[peer, 0, place], 0)
-        return table[code][:5]
-
-    def payload_copy(step):
-        index, device = peer_at(step)
-        return pltpu.make_async_remote_copy(
-            src_ref=payload_out.at[pl.ds(step * CAP, CAP)],
-            dst_ref=payload_in.at[pl.ds(me * CAP, CAP)],
-            send_sem=payload_send.at[step],
-            recv_sem=payload_recv.at[step],
-            device_id=device,
-            device_id_type=MESH,
-        )
-
-    def start_payload(step):
-        index, _ = peer_at(step + 1)
-        for place in range(CAP):
-            payload_out[(step + 1) * CAP + place] = answer(index, place)
-        payload_copy(step + 1).start()
-
-    loop(peers - 1, start_payload)
+    loop(peers * CAP, invert, 8)
 
     for copy in want_copies:
         copy.wait()
@@ -516,10 +523,10 @@
     def regrid(block):
         state_a[block] = pool[new_source[block]]
 
-    loop(SLOTS, regrid)
+    loop(SLOTS, regrid, 2)
 
     def take_face(state, face_id, put):
-        block, face = face_id // 6, lax.rem(face_id, 6)
+        block, face = lax.div(face_id, 6), lax.rem(face_id, 6)
         index = pick_index[face]
         masks = [pick_mask[face, half].reshape(4, 8, 128) for half in range(2)]
         for c in range(5):
@@ -533,14 +540,14 @@
 
     def send_faces(step, state):
         def one(i):
-            side, j = i // 3, lax.rem(i, 3)
+            side, j = (i // 3, i % 3) if isinstance(i, int) else (lax.div(i, 3), lax.rem(i, 3))
 
             def put(c, half, row):
                 faces_out[step][side, j, pl.ds(2 * c + half, 1), :] = row
 
             take_face(state, wants_at[side, 0, j], put)
 
-        loop(6, one)
+        loop(6, one, 3)
         copies = [
             beside_copy(
                 side,
@@ -562,13 +569,13 @@
 
             take_face(state, face_at[r], put)
 
-        loop(FACEREQ, one)
+        loop(FACEREQ, one, 3)
 
     def place_faces(step, state):
         def one(i):
-            side, j = i // 3, lax.rem(i, 3)
+            side, j = (i // 3, i % 3) if isinstance(i, int) else (lax.div(i, 3), lax.rem(i, 3))
             face = lax.rem(wants_out_face(side, j), 6)
-            axis = face // 2
+            axis = lax.div(face, 2)
             index = spread_index[axis].reshape(4, 8, 128)
             odd = (lax.broadcasted_iota(i32, (8, 128), 0) & 1) == 1
             for c in range(5):
@@ -581,7 +588,7 @@
                     parts.append(pick(rows, index[v]))
                 state[SLOTS + i, c] = jnp.concatenate(parts, axis=0)
 
-        loop(6, one)
+        loop(6, one, 3)
 
     def wants_out_face(side, j):
         return face_want[side * 3 + j]
@@ -595,7 +602,7 @@
         row = lax.broadcasted_iota(i32, (16, 128), 0) >> 1
         for r in range(FACEREQ):
             face = lax.rem(face_at[r], 6)
-            axis_row = jnp.where(row == r, face // 2, axis_row)
+            axis_row = jnp.where(row == r, lax.div(face, 2), axis_row)
             sign_row = jnp.where(row == r, (2 * lax.rem(face, 2) - 1).astype(f32), sign_row)
         is_axis = [axis_row == axis for axis in range(3)]
         own = [edge_own[c] for c in range(5)]
@@ -631,7 +638,7 @@
 
     def coarse_ghosts(r):
         slot = request_slot[r]
-        axis = lax.rem(face_at[r], 6) // 2
+        axis = lax.div(lax.rem(face_at[r], 6), 2)
         index = grow_index[axis].reshape(4, 8, 128)
         value = payload_in[slot]
         for when in range(2):
@@ -646,7 +653,7 @@
             state_a[SLOTS + 6 + r, c] = old
             state_b[SLOTS + 6 + r, c] = old + 0.5 * (new - old)
 
-    loop(FACEREQ, coarse_ghosts)
+    loop(FACEREQ, coarse_ghosts, 2)
     register_step(0)
     for copy in copies:
         copy.wait()
@@ -701,7 +708,7 @@
             parcel_out[(step + 1) * 2 + pair] = parcel(index * 2 + pair)
         parcel_copy(step + 1).start()
 
-    loop(peers - 1, start_parcel)
+    loop(peers - 1, start_parcel, 4)
 
     for copy in copies:
         copy.wait()
@@ -716,11 +723,11 @@
     loop(SLOTS, second_step)
 
     def fold(i):
-        c, k = i // 32, lax.rem(i, 32)
+        c, k = lax.div(i, 32), lax.rem(i, 32)
         value = state_c[pl.ds(i, SLOTS, stride=160), :]
         fine_out[c, :, pl.ds(pl.multiple_of(k * 128, 128), 128)] = value
 
-    loop(160, fold)
+    loop(160, fold, 16)
 
     target = lax.broadcasted_iota(i32, (peers, 128), 1)
     wanted = jnp.where(target < 24 * CSLOTS, (target & 3) * 24 + (target >> 2), -7)
@@ -754,7 +761,7 @@
         for pair in range(2):
             gathered[pl.ds(pair * peers + peer, 5, stride=2 * peers), :] = parcel_in[peer * 2 + pair]
 
-    loop(peers, line_up)
+    loop(peers, line_up, 8)
     low8, low4 = (lane8 & 15) < 8, (lane4 & 15) < 8
     for c in range(5):
         value = gathered[pl.ds(c * 2 * peers, 2 * peers), :]
@@ -802,7 +809,7 @@
     peers = sizes[1] * sizes[2]
     smem = pl.BlockSpec(memory_space=pltpu.SMEM)
     vmem = pl.BlockSpec(memory_space=pltpu.VMEM)
-    hbm = pl.BlockSpec(memory_space=pl.ANY)
+    hbm = pl.BlockSpec(memory_space=pltpu.HBM)
     dma = pltpu.SemaphoreType.DMA
     V = pltpu.VMEM
     fine, coarse = pl.pallas_call(

time: 66.5 us -> 52.5 us (0.79)
  Pallas kernels: 59.4 us -> 45.4 us
    pallas_call x1, Pallas kernels: 59.4 us -> 45.4 us  [on_device(): pl.pallas_call(functools.partial(kernel, sizes), out_shape=(jax.ShapeDtyp...]
where the time goes in v1:
time: 52.5 us; the launch traced here: 52.2 us
  Pallas kernels  45.4 us (86%)
  local copies, waits for them, and re-layouts  6.18 us (12%)
  between operations  0.7 us (1%)
    pallas_call x1, Pallas kernels, on_device(): pl.pallas_call(functools.partial(kernel, sizes), out_shape=(jax.ShapeDtyp...  45.4 us
    unnamed x22, local copies, waits for them, and re-layouts  6.18 us

profile of v1, /device:TPU:1, one launch (start us, length us, event | category | flops | bytes accessed | tf_op | source)
XLA Modules:
  0.0 52.2 jit_solution(7807475885785137651)
XLA Ops:
  0.6 0.0 copy-start.4
  0.6 0.0 copy-start.8
  0.7 0.0 copy-start.9
  0.7 0.0 copy-start.5
  0.7 0.0 copy-start.6
  0.7 0.0 copy-start.7
  0.7 0.6 %copy-done.4 = s32[6,6]{1,0:T(8,128)S(1)} copy-done((s32[6,6]{1,0:T(8,128)S(1)}, s32[6,6]{1,0:T(8,128)}, u32[]{:S(2)}) %copy-start.4) | copy-done | bytes 168
  1.3 0.0 copy-done.8
  1.3 0.0 copy-done.9
  1.3 0.0 copy-done.5
  1.3 0.0 copy-done.6
  1.4 0.0 copy-done.7
  1.4 0.0 copy-start
  1.4 1.1 %copy-done = f32[6,5,4096]{2,0,1:T(8,128)S(1)} copy-done((f32[6,5,4096]{2,0,1:T(8,128)S(1)}, f32[6,5,4096]{2,0,1:T(8,128)}, u32[]{:S(2)}) %copy-start) | copy-done | bytes 491544
  2.5 0.0 copy-start.1
  2.5 1.0 %copy-done.1 = f32[4,5,4096]{2,0,1:T(4,128)S(1)} copy-done((f32[4,5,4096]{2,0,1:T(4,128)S(1)}, f32[4,5,4096]{2,0,1:T(4,128)}, u32[]{:S(2)}) %copy-start.1) | copy-done | bytes 327704
  3.4 0.0 copy-start.2
  3.4 1.0 %copy-done.2 = f32[4,5,4096]{2,0,1:T(4,128)S(1)} copy-done((f32[4,5,4096]{2,0,1:T(4,128)S(1)}, f32[4,5,4096]{2,0,1:T(4,128)}, u32[]{:S(2)}) %copy-start.2) | copy-done | bytes 327704
  4.4 0.0 copy-start.3
  4.4 0.9 %copy-done.3 = f32[4,6,5,256]{3,0,2,1:T(4,128)S(1)} copy-done((f32[4,6,5,256]{3,0,2,1:T(4,128)S(1)}, f32[4,6,5,256]{3,0,2,1:T(4,128)}, u32[]{:S(2)}) %copy-start.3) | copy-done | bytes 122904
  5.3 45.4 %shard_map.113 = (f32[5,6,4096]{2,1,0:T(8,128)S(1)}, f32[5,4,4096]{2,1,0:T(4,128)S(1)}) custom-call(s32[2]{0:T(128)S(1)} %copy-done.5, s32[2]{0:T(128)S(1)} %copy-done.6, s32[6]{0:T(128)S(1)} %copy-done.7, s32[6,6]{1,0:T(8,128)S(1)} %copy-done.4, s32[14]{0:T(128)S(1)} %copy-done.8, s32[14]{0:T(128)S(1)} %copy-done.9, f32[5,6,4096]{2,1,0:T(8,128)S(1)} %bitcast.6, ...), custom_call_target="tpu_custom_call" | custom-call | tf_op jit(solution)/shard_map/pallas_call | solution.py:815
  50.7 0.8 %copy.14 = f32[6,5,4096]{2,0,1:T(8,128)} copy(f32[6,5,4096]{2,0,1:T(8,128)S(1)} %bitcast.7) | data formatting | bytes 983040
  51.5 0.7 %copy.15 = f32[4,5,4096]{2,0,1:T(4,128)} copy(f32[4,5,4096]{2,0,1:T(4,128)S(1)} %bitcast.8) | data formatting | bytes 655360
Async XLA Ops:
  0.6 0.7 %copy-start.4 = (s32[6,6]{1,0:T(8,128)S(1)}, s32[6,6]{1,0:T(8,128)}, u32[]{:S(2)}) copy-start(s32[6,6]{1,0:T(8,128)} %face_source.1) | copy-start | bytes 436
  0.6 0.7 %copy-start.8 = (s32[14]{0:T(128)S(1)}, s32[14]{0:T(128)}, u32[]{:S(2)}) copy-start(s32[14]{0:T(128)} %request_slot.1) | copy-start | bytes 172
  0.7 0.7 %copy-start.9 = (s32[14]{0:T(128)S(1)}, s32[14]{0:T(128)}, u32[]{:S(2)}) copy-start(s32[14]{0:T(128)} %request_code.1) | copy-start | bytes 172
  0.7 0.7 %copy-start.5 = (s32[2]{0:T(128)S(1)}, s32[2]{0:T(128)}, u32[]{:S(2)}) copy-start(s32[2]{0:T(128)} %send_left.1) | copy-start | bytes 28
  0.7 0.7 %copy-start.6 = (s32[2]{0:T(128)S(1)}, s32[2]{0:T(128)}, u32[]{:S(2)}) copy-start(s32[2]{0:T(128)} %send_right.1) | copy-start | bytes 28
  0.7 0.7 %copy-start.7 = (s32[6]{0:T(128)S(1)}, s32[6]{0:T(128)}, u32[]{:S(2)}) copy-start(s32[6]{0:T(128)} %new_source.1) | copy-start | bytes 76
  1.4 1.1 %copy-start = (f32[6,5,4096]{2,0,1:T(8,128)S(1)}, f32[6,5,4096]{2,0,1:T(8,128)}, u32[]{:S(2)}) copy-start(f32[6,5,4096]{2,0,1:T(8,128)} %param.10) | copy-start | bytes 1474564
  2.5 1.0 %copy-start.1 = (f32[4,5,4096]{2,0,1:T(4,128)S(1)}, f32[4,5,4096]{2,0,1:T(4,128)}, u32[]{:S(2)}) copy-start(f32[4,5,4096]{2,0,1:T(4,128)} %param.17) | copy-start | bytes 983044
  3.4 1.0 %copy-start.2 = (f32[4,5,4096]{2,0,1:T(4,128)S(1)}, f32[4,5,4096]{2,0,1:T(4,128)}, u32[]{:S(2)}) copy-start(f32[4,5,4096]{2,0,1:T(4,128)} %param.18) | copy-start | bytes 983044
  4.4 0.9 %copy-start.3 = (f32[4,6,5,256]{3,0,2,1:T(4,128)S(1)}, f32[4,6,5,256]{3,0,2,1:T(4,128)}, u32[]{:S(2)}) copy-start(f32[4,6,5,256]{3,0,2,1:T(4,128)} %param.19) | copy-start | bytes 368644

commit v2 on v1

--- a/solution.py
+++ b/solution.py
@@ -201,9 +201,12 @@
     me = gy * n_gz + gz
     rank = gx * peers + me
 
+    at_y = [gy] + [lax.rem(gy + step, n_gy) for step in range(1, n_gy)]
+    at_z = [gz] + [lax.rem(gz + step, n_gz) for step in range(1, n_gz)]
+
     def peer_at(step):
-        index = lax.rem(me + step, peers)
-        return index, (gx, lax.div(index, n_gz), lax.rem(index, n_gz))
+        y, z = at_y[step // n_gz], at_z[step % n_gz]
+        return y * n_gz + z, (gx, y, z)
 
     def on_curve(index):
         return (lax.div(index, peers), lax.rem(lax.div(index, n_gz), n_gy), lax.rem(index, n_gz))
@@ -368,9 +371,10 @@
     loop(224, split_table, 16)
 
     def wait_codes(step):
-        code_copy(step + 1).wait()
-
-    loop(peers - 1, wait_codes)
+        code_copy(step + 1).wait_recv()
+
+    for step in range(peers - 1):
+        wait_codes(step)
     codes_in[me] = codes_out[me]
     to_scalars = pltpu.make_async_copy(codes_in, codes_at, local_sem.at[0])
     to_scalars.start()
@@ -391,13 +395,16 @@
             device_id_type=MESH,
         )
 
-    def start_payload(step):
-        index, _ = peer_at(step + 1)
-        for place in range(CAP):
-            payload_out[(step + 1) * CAP + place] = answer(index, place)
-        payload_copy(step + 1).start()
-
-    loop(peers - 1, start_payload, 4)
+    for first in range(1, peers, 8):
+        group = range(first, min(first + 8, peers))
+        for step in group:
+            index, _ = peer_at(step)
+            for place in range(CAP):
+                payload_out[step * CAP + place] = answer(index, place)
+        for step in group:
+            payload_copy(step).start()
+    for step in range(1, peers):
+        code_copy(step).wait_send()
 
     def scan(i, carry):
         count, wants, places = carry
@@ -498,9 +505,10 @@
             pool[SLOTS + 2 * side + j] = moved[side, j]
 
     def wait_payload(step):
-        payload_copy(step + 1).wait()
-
-    loop(peers - 1, wait_payload)
+        payload_copy(step + 1).wait_recv()
+
+    for step in range(peers - 1):
+        wait_payload(step)
     for place in range(CAP):
         payload_in[me * CAP + place] = answer(me, place)
 
@@ -655,6 +663,8 @@
 
     loop(FACEREQ, coarse_ghosts, 2)
     register_step(0)
+    for step in range(1, peers):
+        payload_copy(step).wait_send()
     for copy in copies:
         copy.wait()
     place_faces(0, state_a)
@@ -702,13 +712,14 @@
         second = average[slot_from[2 * row + 1]]
         return jnp.where((lane5 & 15) < 8, first, second)
 
-    def start_parcel(step):
-        index, _ = peer_at(step + 1)
-        for pair in range(2):
-            parcel_out[(step + 1) * 2 + pair] = parcel(index * 2 + pair)
-        parcel_copy(step + 1).start()
-
-    loop(peers - 1, start_parcel, 4)
+    for first in range(1, peers, 8):
+        group = range(first, min(first + 8, peers))
+        for step in group:
+            index, _ = peer_at(step)
+            for pair in range(2):
+                parcel_out[step * 2 + pair] = parcel(index * 2 + pair)
+        for step in group:
+            parcel_copy(step).start()
 
     for copy in copies:
         copy.wait()
@@ -753,7 +764,8 @@
     def wait_parcel(step):
         parcel_copy(step + 1).wait()
 
-    loop(peers - 1, wait_parcel)
+    for step in range(peers - 1):
+        wait_parcel(step)
     for pair in range(2):
         parcel_in[me * 2 + pair] = parcel(me * 2 + pair)
 
@@ -880,7 +892,7 @@
             dma((peers,)),
         ],
         compiler_params=pltpu.CompilerParams(
-            collective_id=0, has_side_effects=True, vmem_limit_bytes=40 * 1024 * 1024
+            collective_id=0, has_side_effects=True, vmem_limit_bytes=64 * 1024 * 1024
         ),
     )(
         send_left,

time: 52.5 us -> 49.7 us (0.947)
  local copies, waits for them, and re-layouts: 6.18 us -> 2.74 us
  Pallas kernels: 45.4 us -> 46 us
    unnamed x22 -> x4, local copies, waits for them, and re-layouts: 6.18 us -> 2.74 us
    pallas_call x1, Pallas kernels: 45.4 us -> 46 us  [on_device(): pl.pallas_call(functools.partial(kernel, sizes), out_shape=(jax.ShapeDtyp...]
where the time goes in v2:
time: 49.7 us; the launch traced here: 49.4 us
  Pallas kernels  46 us (93%)
  local copies, waits for them, and re-layouts  2.74 us (6%)
  between operations  0.65 us (1%)
    pallas_call x1, Pallas kernels, on_device(): pl.pallas_call(functools.partial(kernel, sizes), out_shape=(jax.ShapeDtyp...  46 us
    unnamed x4, local copies, waits for them, and re-layouts  2.74 us

profile of v2, /device:TPU:1, one launch (start us, length us, event | category | flops | bytes accessed | tf_op | source)
XLA Modules:
  0.0 49.4 jit_solution(2373010961982945460)
XLA Ops:
  0.6 46.0 %shard_map.113 = (f32[5,6,4096]{2,1,0:T(8,128)}, f32[5,4,4096]{2,1,0:T(4,128)}) custom-call(s32[2]{0:T(128)} %send_left.1, s32[2]{0:T(128)} %send_right.1, s32[6]{0:T(128)} %new_source.1, s32[6,6]{1,0:T(8,128)} %face_source.1, s32[14]{0:T(128)} %request_slot.1, s32[14]{0:T(128)} %request_code.1, f32[5,6,4096]{2,1,0:T(8,128)} %bitcast.6, ...), custom_call_target="tpu_custom_call" | custom-call | tf_op jit(solution)/shard_map/pallas_call | solution.py:827
  46.7 0.0 copy-start
  46.7 2.0 %copy.14 = f32[6,5,4096]{2,0,1:T(8,128)} copy(f32[6,5,4096]{2,0,1:T(8,128)} %bitcast.7) | data formatting | bytes 983040
  48.7 0.0 copy-done
  48.7 0.7 %copy.15 = f32[4,5,4096]{2,0,1:T(4,128)} copy(f32[4,5,4096]{2,0,1:T(4,128)S(1)} %bitcast.8) | data formatting | bytes 655360
Async XLA Ops:
  46.7 2.0 %copy-start = (f32[5,4,4096]{2,1,0:T(4,128)S(1)}, f32[5,4,4096]{2,1,0:T(4,128)}, u32[]{:S(2)}) copy-start(f32[5,4,4096]{2,1,0:T(4,128)} %get-tuple-element.5) | copy-start | bytes 983044

commit v3 on v2

--- a/solution.py
+++ b/solution.py
@@ -134,8 +134,8 @@
     old_hbm,
     new_hbm,
     flux_hbm,
-    fine_out,
-    coarse_out,
+    fine_hand,
+    coarse_hand,
     fine_in,
     old_in,
     new_in,
@@ -179,6 +179,9 @@
     parcel_in,
     gathered,
     code_rows,
+    fine_out,
+    coarse_out,
+    store_sem,
     load_sem,
     local_sem,
     code_send,
@@ -242,6 +245,91 @@
     for peer in range(peers):
         codes_out[peer] = code_rows[pl.ds(peer, 1), :]
 
+    def rows_of(block, c):
+        return pl.ds(pl.multiple_of((block * 5 + c) * 32, 32), 32)
+
+    loads[0].wait()
+
+    def unfold(i):
+        c, k = lax.div(i, 32), lax.rem(i, 32)
+        value = fine_in[c, :, pl.ds(pl.multiple_of(k * 128, 128), 128)]
+        own_rows[pl.ds(i, SLOTS, stride=160), :] = value
+
+    loop(160, unfold, 16)
+
+    def split_own(block):
+        for c in range(5):
+            value = own_rows[rows_of(block, c), :]
+            own_flat[block, c] = value
+            pool[block, c] = value
+
+    loop(SLOTS, split_own, 2)
+    for side, listed in enumerate((send_left, send_right)):
+        for j in range(2):
+            bundle[side, j] = own_flat[listed[j]]
+
+    loads[1].wait()
+    loads[2].wait()
+    lane8, lane4 = lane_of(8), lane_of(4)
+
+    def both(c, k):
+        at = pl.ds(k * 128, 128)
+        return old_in[c, :, at], new_in[c, :, at]
+
+    def put_face(c, face, quadrant, value):
+        table_rows[pl.ds((face * 4 + quadrant) * 8 + c, CSLOTS, stride=24 * 8), :] = value
+
+    def fill_table(c):
+        for side in range(2):
+            for half in range(2):
+                first, second = both(c, 30 * side + half)
+                for low, value in enumerate(merge_halves(first, second, 4)):
+                    put_face(c, side, half * 2 + low, value)
+        for side in range(2):
+
+            def fill_y(half, side=side):
+                rows = jnp.zeros((8, 128), f32)
+                for x in range(8):
+                    value = jnp.concatenate(both(c, half * 16 + 2 * x + side), axis=0)
+                    shift = (16 * x - 112 * side) % 128
+                    value = value if shift == 0 else pltpu.roll(value, shift, 1)
+                    rows = jnp.where((lane8 >> 4) == x, value, rows)
+                for low, value in enumerate(merge_halves(rows[:4], rows[4:], 4)):
+                    put_face(c, 2 + side, half * 2 + low, value)
+
+            for half in range(2):
+                fill_y(half)
+
+            def fill_z(quadrant, side=side):
+                rows = jnp.zeros((8, 128), f32)
+                index = (lane8 & 7) * 16 + 15 * side
+                for x in range(8):
+                    k = (quadrant // 2) * 16 + 2 * x + quadrant % 2
+                    value = pick(jnp.concatenate(both(c, k), axis=0), index)
+                    rows = jnp.where((lane8 >> 4) == x, value, rows)
+                put_face(c, 4 + side, quadrant, jnp.where((lane4 & 15) < 8, rows[:4], rows[4:]))
+
+            for quadrant in range(4):
+                fill_z(quadrant)
+
+        def fill_octant(i):
+            half, pair = i // 8, i % 8
+            at = (4 * pair + half) * 128
+            first = old_in[c, :, pl.ds(at, 128)]
+            second = old_in[c, :, pl.ds(at + 256, 128)]
+            for low, value in enumerate(merge_halves(first, second, 4)):
+                code = 96 + ((pair // 4) * 4 + half * 2 + low) * 4 + pair % 4
+                table_rows[pl.ds(code * 8 + c, CSLOTS, stride=32 * 8), :] = value
+
+        for i in range(16):
+            fill_octant(i)
+
+    loop(5, fill_table)
+
+    def split_table(code):
+        table[code] = table_rows[pl.ds(pl.multiple_of(code * 8, 8), 8), :]
+
+    loop(224, split_table, 16)
     pl.semaphore_wait(barrier, peers + 1)
 
     def code_copy(step):
@@ -261,29 +349,6 @@
     for step in range(peers - 1):
         start_codes(step)
 
-    def rows_of(block, c):
-        return pl.ds(pl.multiple_of((block * 5 + c) * 32, 32), 32)
-
-    loads[0].wait()
-
-    def unfold(i):
-        c, k = lax.div(i, 32), lax.rem(i, 32)
-        value = fine_in[c, :, pl.ds(pl.multiple_of(k * 128, 128), 128)]
-        own_rows[pl.ds(i, SLOTS, stride=160), :] = value
-
-    loop(160, unfold, 16)
-
-    def split_own(block):
-        for c in range(5):
-            value = own_rows[rows_of(block, c), :]
-            own_flat[block, c] = value
-            pool[block, c] = value
-
-    loop(SLOTS, split_own, 2)
-    for side, listed in enumerate((send_left, send_right)):
-        for j in range(2):
-            bundle[side, j] = own_flat[listed[j]]
-
     def beside_copy(side, source, target, send, recv):
         return pltpu.make_async_remote_copy(
             src_ref=source,
@@ -307,68 +372,6 @@
     for copy in block_copies:
         copy.start()
 
-    loads[1].wait()
-    loads[2].wait()
-    lane8, lane4 = lane_of(8), lane_of(4)
-
-    def both(c, k):
-        at = pl.ds(k * 128, 128)
-        return old_in[c, :, at], new_in[c, :, at]
-
-    def put_face(c, face, quadrant, value):
-        table_rows[pl.ds((face * 4 + quadrant) * 8 + c, CSLOTS, stride=24 * 8), :] = value
-
-    def fill_table(c):
-        for side in range(2):
-            for half in range(2):
-                first, second = both(c, 30 * side + half)
-                for low, value in enumerate(merge_halves(first, second, 4)):
-                    put_face(c, side, half * 2 + low, value)
-        for side in range(2):
-
-            def fill_y(half, side=side):
-                rows = jnp.zeros((8, 128), f32)
-                for x in range(8):
-                    value = jnp.concatenate(both(c, half * 16 + 2 * x + side), axis=0)
-                    shift = (16 * x - 112 * side) % 128
-                    value = value if shift == 0 else pltpu.roll(value, shift, 1)
-                    rows = jnp.where((lane8 >> 4) == x, value, rows)
-                for low, value in enumerate(merge_halves(rows[:4], rows[4:], 4)):
-                    put_face(c, 2 + side, half * 2 + low, value)
-
-            for half in range(2):
-                fill_y(half)
-
-            def fill_z(quadrant, side=side):
-                rows = jnp.zeros((8, 128), f32)
-                index = (lane8 & 7) * 16 + 15 * side
-                for x in range(8):
-                    k = (quadrant // 2) * 16 + 2 * x + quadrant % 2
-                    value = pick(jnp.concatenate(both(c, k), axis=0), index)
-                    rows = jnp.where((lane8 >> 4) == x, value, rows)
-                put_face(c, 4 + side, quadrant, jnp.where((lane4 & 15) < 8, rows[:4], rows[4:]))
-
-            for quadrant in range(4):
-                fill_z(quadrant)
-
-        def fill_octant(i):
-            half, pair = i // 8, i % 8
-            at = (4 * pair + half) * 128
-            first = old_in[c, :, pl.ds(at, 128)]
-            second = old_in[c, :, pl.ds(at + 256, 128)]
-            for low, value in enumerate(merge_halves(first, second, 4)):
-                code = 96 + ((pair // 4) * 4 + half * 2 + low) * 4 + pair % 4
-                table_rows[pl.ds(code * 8 + c, CSLOTS, stride=32 * 8), :] = value
-
-        for i in range(16):
-            fill_octant(i)
-
-    loop(5, fill_table)
-
-    def split_table(code):
-        table[code] = table_rows[pl.ds(pl.multiple_of(code * 8, 8), 8), :]
-
-    loop(224, split_table, 16)
 
     def wait_codes(step):
         code_copy(step + 1).wait_recv()
@@ -555,7 +558,7 @@
 
             take_face(state, wants_at[side, 0, j], put)
 
-        loop(6, one, 3)
+        loop(6, one, 6)
         copies = [
             beside_copy(
                 side,
@@ -577,7 +580,7 @@
 
             take_face(state, face_at[r], put)
 
-        loop(FACEREQ, one, 3)
+        loop(FACEREQ, one, 6)
 
     def place_faces(step, state):
         def one(i):
@@ -596,7 +599,7 @@
                     parts.append(pick(rows, index[v]))
                 state[SLOTS + i, c] = jnp.concatenate(parts, axis=0)
 
-        loop(6, one, 3)
+        loop(6, one, 6)
 
     def wants_out_face(side, j):
         return face_want[side * 3 + j]
@@ -739,6 +742,8 @@
         fine_out[c, :, pl.ds(pl.multiple_of(k * 128, 128), 128)] = value
 
     loop(160, fold, 16)
+    stores = [pltpu.make_async_copy(fine_out, fine_hand, store_sem.at[5])]
+    stores[0].start()
 
     target = lax.broadcasted_iota(i32, (peers, 128), 1)
     wanted = jnp.where(target < 24 * CSLOTS, (target & 3) * 24 + (target >> 2), -7)
@@ -814,13 +819,38 @@
                     if x_at == 15:
                         value = value + change[1, yh8]
                     coarse_out[c, :, at] = value
+        store = pltpu.make_async_copy(coarse_out.at[c], coarse_hand.at[c], store_sem.at[c])
+        store.start()
+        stores.append(store)
+    for store in stores:
+        store.wait()
+
+
+def hand_over(fine, coarse, fine_out, coarse_out, fine_stage, coarse_stage, in_sem, out_sem):
+    trips = []
+    for c in range(5):
+        for k, (source, stage, target) in enumerate(
+            ((fine, fine_stage, fine_out), (coarse, coarse_stage, coarse_out))
+        ):
+            trips.append(
+                (
+                    pltpu.make_async_copy(source.at[c], stage.at[c], in_sem.at[2 * c + k]),
+                    pltpu.make_async_copy(stage.at[c], target.at[c], out_sem.at[2 * c + k]),
+                )
+            )
+    for arrive, _ in trips:
+        arrive.start()
+    for arrive, leave in trips:
+        arrive.wait()
+        leave.start()
+    for _, leave in trips:
+        leave.wait()
 
 
 def on_device(sizes, fine_old, send_left, send_right, new_source, face_source, request_slot, request_code,
               coarse_old, coarse_new, coarse_flux):
     peers = sizes[1] * sizes[2]
     smem = pl.BlockSpec(memory_space=pltpu.SMEM)
-    vmem = pl.BlockSpec(memory_space=pltpu.VMEM)
     hbm = pl.BlockSpec(memory_space=pltpu.HBM)
     dma = pltpu.SemaphoreType.DMA
     V = pltpu.VMEM
@@ -831,7 +861,7 @@
             jax.ShapeDtypeStruct((5, CSLOTS, 4096), f32),
         ),
         in_specs=[smem] * 6 + [hbm] * 4,
-        out_specs=(vmem, vmem),
+        out_specs=(hbm, hbm),
         scratch_shapes=[
             V((5, SLOTS, 4096), f32),
             V((5, CSLOTS, 4096), f32),
@@ -876,6 +906,9 @@
             V((peers * 2, 5, 128), f32),
             V((8 * 2 * peers, 128), f32),
             V((peers, 128), i32),
+            V((5, SLOTS, 4096), f32),
+            V((5, CSLOTS, 4096), f32),
+            dma((6,)),
             dma((4,)),
             dma((2,)),
             dma((peers,)),
@@ -906,6 +939,22 @@
         jnp.transpose(coarse_new, (1, 0, 2)),
         jnp.transpose(coarse_flux, (1, 2, 0, 3)),
     )
+    fine, coarse = pl.pallas_call(
+        hand_over,
+        out_shape=(
+            jax.ShapeDtypeStruct((5, SLOTS, 4096), f32),
+            jax.ShapeDtypeStruct((5, CSLOTS, 4096), f32),
+        ),
+        in_specs=[hbm, hbm],
+        out_specs=(hbm, hbm),
+        scratch_shapes=[
+            V((5, SLOTS, 4096), f32),
+            V((5, CSLOTS, 4096), f32),
+            dma((10,)),
+            dma((10,)),
+        ],
+        compiler_params=pltpu.CompilerParams(vmem_limit_bytes=64 * 1024 * 1024),
+    )(fine, coarse)
     return jnp.transpose(fine, (1, 0, 2)), jnp.transpose(coarse, (1, 0, 2))
 
 

time: 49.7 us -> 48.9 us (0.984)
  local copies, waits for them, and re-layouts: 2.74 us -> 0 us
  Pallas kernels: 46 us -> 48.1 us
    unnamed x4 -> x0, local copies, waits for them, and re-layouts: 2.74 us -> none
    pallas_call x0 -> x1, Pallas kernels: none -> 2.1 us  [on_device(): pl.pallas_call(hand_over, out_shape=(jax.ShapeDtypeStruct((5, SLOTS, 4096...]
where the time goes in v3:
time: 48.9 us; the launch traced here: 48.8 us
  Pallas kernels  48.1 us (98%)
  between operations  0.64 us (1%)
    pallas_call x1, Pallas kernels, on_device(): pl.pallas_call(functools.partial(kernel, sizes), out_shape=(jax.ShapeDtyp...  46 us
    pallas_call x1, Pallas kernels, on_device(): pl.pallas_call(hand_over, out_shape=(jax.ShapeDtypeStruct((5, SLOTS, 4096...  2.1 us

profile of v3, /device:TPU:1, one launch (start us, length us, event | category | flops | bytes accessed | tf_op | source)
XLA Modules:
  0.0 48.8 jit_solution(2495636482302273514)
XLA Ops:
  0.6 46.0 %shard_map.113 = (f32[5,6,4096]{2,1,0:T(8,128)}, f32[5,4,4096]{2,1,0:T(4,128)}) custom-call(s32[2]{0:T(128)} %send_left.1, s32[2]{0:T(128)} %send_right.1, s32[6]{0:T(128)} %new_source.1, s32[6,6]{1,0:T(8,128)} %face_source.1, s32[14]{0:T(128)} %request_slot.1, s32[14]{0:T(128)} %request_code.1, f32[5,6,4096]{2,1,0:T(8,128)} %bitcast.6, ...), custom_call_target="tpu_custom_call" | custom-call | tf_op jit(solution)/shard_map/pallas_call | solution.py:857
  46.7 2.1 %shard_map.114 = (f32[5,6,4096]{2,1,0:T(8,128)}, f32[5,4,4096]{2,1,0:T(4,128)}) custom-call(f32[5,6,4096]{2,1,0:T(8,128)} %get-tuple-element.6.fine, f32[5,4,4096]{2,1,0:T(4,128)} %get-tuple-element.7.coarse), custom_call_target="tpu_custom_call" | custom-call | tf_op jit(solution)/shard_map/pallas_call | solution.py:942

commit v4 on v3

--- a/solution.py
+++ b/solution.py
@@ -330,85 +330,6 @@
         table[code] = table_rows[pl.ds(pl.multiple_of(code * 8, 8), 8), :]
 
     loop(224, split_table, 16)
-    pl.semaphore_wait(barrier, peers + 1)
-
-    def code_copy(step):
-        index, device = peer_at(step)
-        return pltpu.make_async_remote_copy(
-            src_ref=codes_out.at[index],
-            dst_ref=codes_in.at[me],
-            send_sem=code_send.at[step],
-            recv_sem=code_recv.at[step],
-            device_id=device,
-            device_id_type=MESH,
-        )
-
-    def start_codes(step):
-        code_copy(step + 1).start()
-
-    for step in range(peers - 1):
-        start_codes(step)
-
-    def beside_copy(side, source, target, send, recv):
-        return pltpu.make_async_remote_copy(
-            src_ref=source,
-            dst_ref=target,
-            send_sem=send,
-            recv_sem=recv,
-            device_id=beside[side],
-            device_id_type=MESH,
-        )
-
-    block_copies = [
-        beside_copy(
-            side,
-            bundle.at[side],
-            moved.at[1 - side],
-            block_send.at[side],
-            block_recv.at[1 - side],
-        )
-        for side in range(2)
-    ]
-    for copy in block_copies:
-        copy.start()
-
-
-    def wait_codes(step):
-        code_copy(step + 1).wait_recv()
-
-    for step in range(peers - 1):
-        wait_codes(step)
-    codes_in[me] = codes_out[me]
-    to_scalars = pltpu.make_async_copy(codes_in, codes_at, local_sem.at[0])
-    to_scalars.start()
-    to_scalars.wait()
-
-    def answer(peer, place):
-        code = jnp.maximum(codes_at[peer, 0, place], 0)
-        return table[code][:5]
-
-    def payload_copy(step):
-        index, device = peer_at(step)
-        return pltpu.make_async_remote_copy(
-            src_ref=payload_out.at[pl.ds(step * CAP, CAP)],
-            dst_ref=payload_in.at[pl.ds(me * CAP, CAP)],
-            send_sem=payload_send.at[step],
-            recv_sem=payload_recv.at[step],
-            device_id=device,
-            device_id_type=MESH,
-        )
-
-    for first in range(1, peers, 8):
-        group = range(first, min(first + 8, peers))
-        for step in group:
-            index, _ = peer_at(step)
-            for place in range(CAP):
-                payload_out[step * CAP + place] = answer(index, place)
-        for step in group:
-            payload_copy(step).start()
-    for step in range(1, peers):
-        code_copy(step).wait_send()
-
     def scan(i, carry):
         count, wants, places = carry
         e = face_source[lax.div(i, 6), lax.rem(i, 6)]
@@ -456,14 +377,6 @@
             found = jnp.where(request_slot[r] == slot, r, found)
         slot_from[slot] = found
 
-    want_copies = [
-        beside_copy(
-            side, wants_out.at[side], wants_in.at[1 - side], want_send.at[side], want_recv.at[1 - side]
-        )
-        for side in range(2)
-    ]
-    for copy in want_copies:
-        copy.start()
     sub = lax.broadcasted_iota(i32, (32, 128), 0)
     lane = lax.broadcasted_iota(i32, (32, 128), 1)
     x, yh = sub >> 1, sub & 1
@@ -493,6 +406,93 @@
     grow_index[2] = (x >> 1) * 16 + 4 * yh + (lane >> 5)
 
     loop(peers * CAP, invert, 8)
+    pl.semaphore_wait(barrier, peers + 1)
+
+    def code_copy(step):
+        index, device = peer_at(step)
+        return pltpu.make_async_remote_copy(
+            src_ref=codes_out.at[index],
+            dst_ref=codes_in.at[me],
+            send_sem=code_send.at[step],
+            recv_sem=code_recv.at[step],
+            device_id=device,
+            device_id_type=MESH,
+        )
+
+    def start_codes(step):
+        code_copy(step + 1).start()
+
+    for step in range(peers - 1):
+        start_codes(step)
+
+    def beside_copy(side, source, target, send, recv):
+        return pltpu.make_async_remote_copy(
+            src_ref=source,
+            dst_ref=target,
+            send_sem=send,
+            recv_sem=recv,
+            device_id=beside[side],
+            device_id_type=MESH,
+        )
+
+    want_copies = [
+        beside_copy(
+            side, wants_out.at[side], wants_in.at[1 - side], want_send.at[side], want_recv.at[1 - side]
+        )
+        for side in range(2)
+    ]
+    for copy in want_copies:
+        copy.start()
+    block_copies = [
+        beside_copy(
+            side,
+            bundle.at[side],
+            moved.at[1 - side],
+            block_send.at[side],
+            block_recv.at[1 - side],
+        )
+        for side in range(2)
+    ]
+    for copy in block_copies:
+        copy.start()
+
+
+    def wait_codes(step):
+        code_copy(step + 1).wait_recv()
+
+    for step in range(peers - 1):
+        wait_codes(step)
+    codes_in[me] = codes_out[me]
+    to_scalars = pltpu.make_async_copy(codes_in, codes_at, local_sem.at[0])
+    to_scalars.start()
+    to_scalars.wait()
+
+    def answer(peer, place):
+        code = jnp.maximum(codes_at[peer, 0, place], 0)
+        return table[code][:5]
+
+    def payload_copy(step):
+        index, device = peer_at(step)
+        return pltpu.make_async_remote_copy(
+            src_ref=payload_out.at[pl.ds(step * CAP, CAP)],
+            dst_ref=payload_in.at[pl.ds(me * CAP, CAP)],
+            send_sem=payload_send.at[step],
+            recv_sem=payload_recv.at[step],
+            device_id=device,
+            device_id_type=MESH,
+        )
+
+    for first in range(1, peers, 8):
+        group = range(first, min(first + 8, peers))
+        for step in group:
+            index, _ = peer_at(step)
+            for place in range(CAP):
+                payload_out[step * CAP + place] = answer(index, place)
+        for step in group:
+            payload_copy(step).start()
+    for step in range(1, peers):
+        code_copy(step).wait_send()
+
 
     for copy in want_copies:
         copy.wait()

time: 48.9 us -> 50.8 us (1.039)
  Pallas kernels: 48.1 us -> 50 us
    pallas_call x1, Pallas kernels: 46 us -> 47.9 us  [on_device(): pl.pallas_call(functools.partial(kernel, sizes), out_shape=(jax.ShapeDtyp...]
where the time goes in v4:
time: 50.8 us; the launch traced here: 50.6 us
  Pallas kernels  50 us (98%)
  between operations  0.64 us (1%)
    pallas_call x1, Pallas kernels, on_device(): pl.pallas_call(functools.partial(kernel, sizes), out_shape=(jax.ShapeDtyp...  47.9 us
    pallas_call x1, Pallas kernels, on_device(): pl.pallas_call(hand_over, out_shape=(jax.ShapeDtypeStruct((5, SLOTS, 4096...  2.1 us

profile of v4, /device:TPU:1, one launch (start us, length us, event | category | flops | bytes accessed | tf_op | source)
XLA Modules:
  0.0 50.6 jit_solution(9008750652193409615)
XLA Ops:
  0.6 47.9 %shard_map.113 = (f32[5,6,4096]{2,1,0:T(8,128)}, f32[5,4,4096]{2,1,0:T(4,128)}) custom-call(s32[2]{0:T(128)} %send_left.1, s32[2]{0:T(128)} %send_right.1, s32[6]{0:T(128)} %new_source.1, s32[6,6]{1,0:T(8,128)} %face_source.1, s32[14]{0:T(128)} %request_slot.1, s32[14]{0:T(128)} %request_code.1, f32[5,6,4096]{2,1,0:T(8,128)} %bitcast.6, ...), custom_call_target="tpu_custom_call" | custom-call | tf_op jit(solution)/shard_map/pallas_call | solution.py:857
  48.5 2.1 %shard_map.114 = (f32[5,6,4096]{2,1,0:T(8,128)}, f32[5,4,4096]{2,1,0:T(4,128)}) custom-call(f32[5,6,4096]{2,1,0:T(8,128)} %get-tuple-element.6.fine, f32[5,4,4096]{2,1,0:T(4,128)} %get-tuple-element.7.coarse), custom_call_target="tpu_custom_call" | custom-call | tf_op jit(solution)/shard_map/pallas_call | solution.py:942
